TPU v7x, 256 devices: a whole 4x4x8 slice. The times are simulated.
256 devices in a mesh: seq: 32 (over y, z), head: 8 (over x, core).
Axes of the slice: x: 4, y: 4, z: 8, core: 2. Of those that a mesh axis runs over, the one named last changes fastest.
Arguments:
- queries: bfloat16 [32768, 4096], P('seq', 'head'), may hold values from -6 to 6
- keys: bfloat16 [32768, 4096], P('seq', 'head'), may hold values from -6 to 6
- values: bfloat16 [32768, 4096], P('seq', 'head'), may hold values from -6.6 to 6.6, as said below
- d_normed: bfloat16 [32768, 4096], P('seq', 'head'), may hold values from -6 to 6
- gain: float32 [4096], P('head'), may hold values from 0.1 to 1.9
Outputs:
- d_queries: bfloat16 [32768, 4096], P('seq', 'head')
- d_keys: bfloat16 [32768, 4096], P('seq', 'head')
- d_values: bfloat16 [32768, 4096], P('seq', 'head')
Inputs may be any that keep to these rules, and one draw needn't show every extreme that they name: `values`: entries are bounded.
All inputs are finite; a program needn't handle non-finite values.
Results may differ from a plain program's by a relative error of at most 0.0058.
Values sent between devices are 32-bit elements; how exact they have to be, the bound alone decides.
A program may use at most 128 MiB of HBM per device.

v0:
```python
import jax
import jax.numpy as jnp
from jax import lax
from jax.sharding import PartitionSpec as P

HD = 128


eps = 1e-06


def local(queries, keys, values, d_normed, gain):
    tok_rows, feat_width = queries.shape
    head_count = feat_width // HD
    later_pos = lax.broadcasted_iota(jnp.int32, (tok_rows, tok_rows), 0)
    earlier_pos = lax.broadcasted_iota(jnp.int32, (tok_rows, tok_rows), 1)
    causal = later_pos >= earlier_pos
    my_index = lax.axis_index("seq")
    query3 = queries.reshape(tok_rows, head_count, HD)
    key_tensor3 = keys.reshape(tok_rows, head_count, HD)
    value_tensor3 = values.reshape(tok_rows, head_count, HD)
    local_key_value = jnp.einsum(
        "iap,iaq->apq", key_tensor3, value_tensor3, preferred_element_type=jnp.float32
    )
    shard_part = lax.all_gather(local_key_value[None], "seq", axis=0, tiled=True)
    positions = jnp.arange(shard_part.shape[0], dtype=jnp.int32)
    weight = (positions < my_index).astype(jnp.float32)
    kv_before = jnp.sum(shard_part * weight[:, None, None, None], axis=0)
    kv_low = kv_before.astype(jnp.bfloat16)

    def columns(array, head_index):
        return array[:, head_index * HD : (head_index + 1) * HD]

    score_list = []
    output_list = []
    for head_index in range(head_count):
        query_cols = columns(queries, head_index)
        key_cols = columns(keys, head_index)
        value_cols = columns(values, head_index)
        raw_scores = jnp.dot(query_cols, key_cols.T, preferred_element_type=jnp.float32)
        score_matrix = jnp.where(causal, raw_scores, 0.0).astype(jnp.bfloat16)
        score_list.append(score_matrix)
        head_out = jnp.dot(score_matrix, value_cols, preferred_element_type=jnp.float32)
        head_out = head_out + jnp.dot(
            query_cols, kv_low[head_index], preferred_element_type=jnp.float32
        )
        output_list.append(head_out)
    attended_rows = jnp.concatenate(output_list, axis=1)
    scaled = d_normed.astype(jnp.float32) * gain[None, :]
    total_sq, total_cross = lax.psum(
        (jnp.sum(attended_rows * attended_rows, axis=1), jnp.sum(scaled * attended_rows, axis=1)),
        "head",
    )
    features = feat_width * lax.axis_size("head")
    inv_rms = lax.rsqrt(total_sq / features + eps)
    cross_mean = total_cross / features
    d_attended = (
        inv_rms[:, None] * scaled - attended_rows * (inv_rms**3 * cross_mean)[:, None]
    ).astype(jnp.bfloat16)
    own_grad = jnp.einsum(
        "iap,iaq->apq",
        query3,
        d_attended.reshape(tok_rows, head_count, HD),
        preferred_element_type=jnp.float32,
    )
    shard_part = lax.all_gather(own_grad[None], "seq", axis=0, tiled=True)
    positions = jnp.arange(shard_part.shape[0], dtype=jnp.int32)
    weight = (positions > my_index).astype(jnp.float32)
    grad_after = jnp.sum(shard_part * weight[:, None, None, None], axis=0)
    grad_low = grad_after.astype(jnp.bfloat16)
    query_grads = []
    key_grads = []
    value_grads = []
    for head_index in range(head_count):
        query_cols = columns(queries, head_index)
        key_cols = columns(keys, head_index)
        value_cols = columns(values, head_index)
        d_att_cols = columns(d_attended, head_index)
        raw_grad = jnp.dot(d_att_cols, value_cols.T, preferred_element_type=jnp.float32)
        score_gradient = jnp.where(causal, raw_grad, 0.0).astype(jnp.bfloat16)
        query_gradient = jnp.dot(score_gradient, key_cols, preferred_element_type=jnp.float32)
        query_gradient = query_gradient + jnp.dot(
            d_att_cols, kv_low[head_index].T, preferred_element_type=jnp.float32
        )
        key_gradient = jnp.dot(score_gradient.T, query_cols, preferred_element_type=jnp.float32)
        key_gradient = key_gradient + jnp.dot(
            value_cols, grad_low[head_index].T, preferred_element_type=jnp.float32
        )
        value_gradient = jnp.dot(
            score_list[head_index].T, d_att_cols, preferred_element_type=jnp.float32
        )
        value_gradient = value_gradient + jnp.dot(
            key_cols, grad_low[head_index], preferred_element_type=jnp.float32
        )
        query_grads.append(query_gradient.astype(jnp.bfloat16))
        key_grads.append(key_gradient.astype(jnp.bfloat16))
        value_grads.append(value_gradient.astype(jnp.bfloat16))
    return (
        jnp.concatenate(query_grads, axis=1),
        jnp.concatenate(key_grads, axis=1),
        jnp.concatenate(value_grads, axis=1),
    )


def solution(mesh):
    in_specs = (P("seq", "head"), P("seq", "head"), P("seq", "head"), P("seq", "head"), P("head"))
    out_specs = (P("seq", "head"), P("seq", "head"), P("seq", "head"))
    return jax.shard_map(local, mesh=mesh, in_specs=in_specs, out_specs=out_specs, check_vma=False)
```

profile of v0, /device:TPU:1, one launch (start us, length us, event | category | flops | bytes accessed | tf_op | source)
XLA Modules:
  0.0 259.0 jit_solution(14285045564201152050)
XLA Ops:
  7.2 2.3 copy.24
  9.6 2.5 fusion.26
  12.2 1.5 copy.17
  13.7 0.7 select_convert_fusion.5
  14.5 0.7 select_convert_fusion.6
  15.2 0.8 select_convert_fusion.7
  16.0 0.7 select_convert_fusion.4
  16.8 1.2 copy-done.23
  17.9 0.8 fusion.59
  18.8 1.6 fusion.71
  20.4 1.6 fusion.83
  22.0 1.6 fusion.47
  23.6 90.5 %all-gather.5.cloned.1.call-done = f32[128,128,128]{2,1,0:T(8,128)} async-done(((f32[4,128,128]{2,1,0:T(8,128)}), f32[128,128,128]{2,1,0:T(8,128)}) %all-gather.5.cloned.1.call-update) | async-done | bytes 8388624 | tf_op jit(solution)/shard_map/all_gather | solution.py:25
  114.2 4.4 %multiply_reduce_fusion.1 = bf16[4,128,128]{2,1,0:T(8,128)(2,1)S(1)} fusion(f32[32,4,128,128]{3,2,1,0:T(8,128)} %bitcast.136, f32[32]{0:T(128)S(1)} %compare_convert_fusion.1), kind=kLoop, calls=%fused_computation.1 | loop fusion | flops 4128768 | bytes 8519808 | tf_op jit(solution)/shard_map/reduce_sum | solution.py:28
  119.1 0.5 copy-done.34
  120.9 13.2 %all-reduce = (f32[1024]{0:T(1024)S(1)}, f32[1024]{0:T(1024)S(1)}) all-reduce(f32[1024]{0:T(1024)S(1)} %get-tuple-element.10, f32[1024]{0:T(1024)S(1)} %get-tuple-element.9), channel_id=1, replica_groups=mesh['seq'=32,'head'=8] {'head'}, use_global_device_ids=true, to_apply=%region_4.5 | all-reduce | flops 2048 | bytes 16384 | tf_op jit(solution)/shard_map/psum | solution.py:50
  134.2 1.7 subtract_convert_fusion
  135.9 1.0 copy-done.7
  137.3 0.8 copy.19
  138.2 1.8 select_convert_fusion
  140.1 0.8 fusion.50
  141.6 0.8 select_convert_fusion.1
  142.4 0.8 fusion.62
  143.5 0.8 select_convert_fusion.2
  144.3 0.8 fusion.74
  145.3 0.8 select_convert_fusion.3
  146.1 0.8 fusion.86
  147.7 1.0 pad_maximum_fusion.1
  148.7 2.3 copy.21
  151.0 3.0 %fusion.42 = f32[1024,128]{0,1:T(8,128)} fusion(bf16[1024,1024]{1,0:T(8,128)(2,1)} %copy-done.15, bf16[1024,512]{0,1:T(8,128)(2,1)} %copy-done.7), kind=kOutput, calls=%fused_computation.78 | convolution fusion | flops 268435456 | bytes 2883584 | tf_op jit(solution)/shard_map/dot_general | solution.py:89
  154.0 3.0 %fusion.38 = f32[1024,128]{0,1:T(8,128)} fusion(bf16[1024,1024]{1,0:T(8,128)(2,1)} %copy-done.14, bf16[1024,512]{0,1:T(8,128)(2,1)S(1)} %copy-done.9), kind=kOutput, calls=%fused_computation.74 | convolution fusion | flops 268435456 | bytes 2883584 | tf_op jit(solution)/shard_map/dot_general | solution.py:89
  157.1 1.3 fusion.34
  158.3 0.5 copy-done.13
  158.8 1.2 fusion.30
  160.1 1.3 fusion.53
  161.4 0.5 copy-done.1
  161.9 0.5 fusion.65
  162.4 1.1 copy-done.3
  163.5 1.3 fusion.77
  164.8 0.5 copy-done.5
  165.3 1.3 fusion.89
  166.6 66.2 %all-gather.7.cloned.1.call-done = f32[128,128,128]{2,1,0:T(8,128)} async-done(((f32[4,128,128]{2,1,0:T(8,128)}), f32[128,128,128]{2,1,0:T(8,128)}) %all-gather.7.cloned.1.call-update) | async-done | bytes 8388624 | tf_op jit(solution)/shard_map/all_gather | solution.py:66
  232.8 9.0 %copy.20 = f32[32,4,128,128]{2,3,1,0:T(8,128)} copy(f32[32,4,128,128]{3,2,1,0:T(8,128)} %bitcast.135) | data formatting | bytes 16777216 | tf_op jit(solution)/shard_map/all_gather | solution.py:66
  241.8 4.3 %multiply_reduce_fusion = bf16[4,128,128]{1,2,0:T(8,128)(2,1)S(1)} fusion(f32[32,4,128,128]{2,3,1,0:T(8,128)} %copy.20, f32[32]{0:T(128)S(1)} %compare_convert_fusion), kind=kLoop, calls=%fused_computation | loop fusion | flops 4128768 | bytes 8519808 | tf_op jit(solution)/shard_map/reduce_sum | solution.py:69
  246.7 0.5 copy-done.29
  247.8 1.3 copy.23
  249.7 0.5 copy-done.27
  250.8 1.3 copy.22
  (92 shorter events, 6.4 us)
Async XLA Ops:
  7.2 2.4 copy-start.22
  7.2 107.0 %all-gather.5.cloned.1.call-start = ((), (), s32[]{:S(2)}) async-start(), calls=%async_computation | async-start | bytes 8650752 | tf_op jit(solution)/shard_map/all_gather | solution.py:25
  9.6 4.1 %copy-start.6 = (bf16[1024,512]{1,0:T(8,128)(2,1)S(1)}, bf16[1024,512]{1,0:T(8,128)(2,1)}, u32[]{:S(2)}) copy-start(bf16[1024,512]{1,0:T(8,128)(2,1)} %param.6) | copy-start | bytes 3145732
  9.6 4.1 %copy-start.18 = (bf16[1024,512]{1,0:T(8,128)(2,1)S(1)}, bf16[1024,512]{1,0:T(8,128)(2,1)}, u32[]{:S(2)}) copy-start(bf16[1024,512]{1,0:T(8,128)(2,1)} %param.5) | copy-start | bytes 3145732
  12.1 220.7 %all-gather.7.cloned.1.call-start = ((), (), s32[]{:S(2)}) async-start(), calls=%async_computation.1 | async-start | bytes 8650752 | tf_op jit(solution)/shard_map/all_gather | solution.py:66
  14.5 2.3 copy-start.10
  15.2 3.5 %copy-start.14 = (bf16[1024,1024]{1,0:T(8,128)(2,1)}, bf16[1024,1024]{1,0:T(8,128)(2,1)S(1)}, u32[]{:S(2)}) copy-start(bf16[1024,1024]{1,0:T(8,128)(2,1)S(1)} %select_convert_fusion.6) | copy-start | bytes 6291460
  16.0 4.4 %copy-start.15 = (bf16[1024,1024]{1,0:T(8,128)(2,1)}, bf16[1024,1024]{1,0:T(8,128)(2,1)S(1)}, u32[]{:S(2)}) copy-start(bf16[1024,1024]{1,0:T(8,128)(2,1)S(1)} %select_convert_fusion.7) | copy-start | bytes 6291460
  16.0 1.9 copy-start.23
  17.9 4.1 %copy-start.12 = (bf16[1024,1024]{1,0:T(8,128)(2,1)}, bf16[1024,1024]{1,0:T(8,128)(2,1)S(1)}, u32[]{:S(2)}) copy-start(bf16[1024,1024]{1,0:T(8,128)(2,1)S(1)} %select_convert_fusion.4) | copy-start | bytes 6291460
  114.2 4.4 %copy-start.19 = (bf16[1024,512]{1,0:T(8,128)(2,1)S(1)}, bf16[1024,512]{1,0:T(8,128)(2,1)}, u32[]{:S(2)}) copy-start(bf16[1024,512]{1,0:T(8,128)(2,1)} %param.5) | copy-start | bytes 3145732
  114.2 4.7 %copy-start.35 = (f32[1024,128]{0,1:T(8,128)S(1)}, f32[1024,128]{0,1:T(8,128)}, u32[]{:S(2)}) copy-start(f32[1024,128]{0,1:T(8,128)} %fusion.71) | copy-start | bytes 1572868
  118.6 1.0 copy-start.34
  118.6 1.3 copy-start.33
  118.9 1.3 copy-start.36
  119.9 0.8 copy-start.16
  120.1 0.8 copy-start.17
  134.2 2.7 %copy-start.20 = (bf16[1024,512]{1,0:T(8,128)(2,1)S(1)}, bf16[1024,512]{1,0:T(8,128)(2,1)}, u32[]{:S(2)}) copy-start(bf16[1024,512]{1,0:T(8,128)(2,1)} %param.5) | copy-start | bytes 3145732
  135.9 1.0 copy-start.7
  140.0 1.2 copy-start.8
  140.0 1.5 copy-start.24
  142.4 1.9 copy-start
  144.3 1.9 copy-start.2
  146.1 1.3 copy-start.4
  151.0 3.0 %copy-start.9 = (bf16[1024,512]{0,1:T(8,128)(2,1)S(1)}, bf16[1024,512]{0,1:T(8,128)(2,1)}, u32[]{:S(2)}) copy-start(bf16[1024,512]{0,1:T(8,128)(2,1)} %copy-done.7) | copy-start | bytes 3145732
  154.0 3.0 %copy-start.11 = (bf16[1024,1024]{1,0:T(8,128)(2,1)S(1)}, bf16[1024,1024]{1,0:T(8,128)(2,1)}, u32[]{:S(2)}) copy-start(bf16[1024,1024]{1,0:T(8,128)(2,1)} %copy-done.10) | copy-start | bytes 6291460
  157.1 1.8 copy-start.13
  158.8 1.2 copy-start.21
  160.1 1.8 copy-start.1
  161.9 1.6 copy-start.3
  163.5 1.8 copy-start.5
  241.8 4.3 %copy-start.32 = (f32[1024,128]{0,1:T(8,128)S(1)}, f32[1024,128]{0,1:T(8,128)}, u32[]{:S(2)}) copy-start(f32[1024,128]{0,1:T(8,128)} %fusion.34) | copy-start | bytes 1572868
  241.8 4.6 %copy-start.30 = (f32[1024,128]{0,1:T(8,128)S(1)}, f32[1024,128]{0,1:T(8,128)}, u32[]{:S(2)}) copy-start(f32[1024,128]{0,1:T(8,128)} %fusion.38) | copy-start | bytes 1572868
  246.1 1.0 copy-start.29
  246.2 1.3 copy-start.31
  247.7 1.4 copy-start.25
  247.7 1.5 copy-start.26
  249.2 1.0 copy-start.27
  249.2 1.3 copy-start.28
Sparse Core Ops, SparseCore 0:
  12.2 101.8 all-gather.4
  138.3 94.4 all-gather.6
where the time goes:
time: 260 us; the launch traced here: 259 us
  waiting for transfers between devices  157 us (60%)
  matrix products  35.8 us (14%)
  local copies, waits for them, and re-layouts  26.3 us (10%)
  between operations  14.6 us (6%)
  blocking collectives  13.2 us (5%)
  other arithmetic  12.1 us (5%)
    all_gather x1, waiting for transfers between devices, local(): lax.all_gather(local_key_value[None], 'seq', axis=0, tiled=True)  90.5 us
    all_gather x1, waiting for transfers between devices, local(): shard_part = lax.all_gather(own_grad[None], 'seq', axis=0, tiled=True)  66.2 us
    unnamed x78, local copies, waits for them, and re-layouts  14.2 us
    psum x1, blocking collectives, local(): lax.psum((jnp.sum(attended_rows * attended_rows, axis=1), jnp.sum(scaled...  13.2 us
    all_gather x1, local copies, waits for them, and re-layouts, local(): shard_part = lax.all_gather(own_grad[None], 'seq', axis=0, tiled=True)  8.96 us
    dot_general x4, matrix products, local(): jnp.dot(score_list[head_index].T, d_att_cols, preferred_element_type=jnp....  8.54 us
    dot_general x4, matrix products, local(): jnp.dot(score_matrix, value_cols, preferred_element_type=jnp.float32)  5.69 us
  transfers between devices with their start and end apart: 2, of which 2 were waited for; matrix products, arithmetic and copies ran while one was open for 13% of the time, Pallas kernels for 0%

commit v1 on v0

v1 whole, which is shorter than its diff:
```python
import functools

import jax
import jax.numpy as jnp
from jax import lax
from jax.experimental import pallas as pl
from jax.experimental.pallas import tpu as pltpu
from jax.sharding import PartitionSpec as P

MESH = pl.DeviceIdType.MESH
HD = 128
BLK = 256
eps = 1e-06
f32 = jnp.float32
bf16 = jnp.bfloat16

NN = (((1,), (0,)), ((), ()))
NT = (((1,), (1,)), ((), ()))
TN = (((0,), (0,)), ((), ()))


def dot(a, b, dims=NN):
    return lax.dot_general(a, b, dims, preferred_element_type=f32)


def thirds(x):
    hi = x.astype(bf16)
    rest = x - hi.astype(f32)
    mid = rest.astype(bf16)
    low = (rest - mid.astype(f32)).astype(bf16)
    return hi, mid, low


def kernel(
    n_seq, n_head,
    q_hbm, k_hbm, v_hbm, dn_hbm, gain_ref,
    dq_hbm, dk_hbm, dv_hbm,
    q, k, v, dn, qt, st, att, da, own, up, pre, kvb, kvlow, own2, up2, pre2, gb, dk_part, dv_part,
    dq_o, dk_o, dv_o, stat, stat_in,
    in_sem, out_sem, up_s, up_r, down_s, down_r, up2_s, up2_r, down2_s, down2_r, stat_s, stat_r, loc_sem,
):
    toks, feat = q.shape
    heads = feat // HD
    nb = toks // BLK
    rows = own.shape[0] // n_seq
    seq = lax.axis_index("seq")
    head = lax.axis_index("head")

    loads = [
        pltpu.make_async_copy(src, dst, in_sem.at[i])
        for i, (src, dst) in enumerate(((k_hbm, k), (v_hbm, v), (q_hbm, q), (dn_hbm, dn)))
    ]
    for c in loads:
        c.start()

    barrier = pltpu.get_barrier_semaphore()

    def greet_seq(d, _):
        pl.semaphore_signal(barrier, inc=1, device_id={"seq": lax.rem(seq + d, n_seq)}, device_id_type=MESH)
        return 0

    def greet_head(d, _):
        pl.semaphore_signal(barrier, inc=1, device_id={"head": lax.rem(head + d, n_head)}, device_id_type=MESH)
        return 0

    lax.fori_loop(1, n_seq, greet_seq, 0)
    lax.fori_loop(1, n_head, greet_head, 0)

    def cols(h):
        return slice(h * HD, (h + 1) * HD)

    def scatter(src, dst, send, recv):
        def step(d, _):
            peer = lax.rem(seq + d, n_seq)
            pltpu.make_async_remote_copy(
                src_ref=src.at[pl.ds(pl.multiple_of(peer * rows, rows), rows)],
                dst_ref=dst.at[pl.ds(pl.multiple_of(seq * rows, rows), rows)],
                send_sem=send, recv_sem=recv, device_id={"seq": peer}, device_id_type=MESH,
            ).start()
            return 0

        lax.fori_loop(1, n_seq, step, 0)
        mine = pl.ds(pl.multiple_of(seq * rows, rows), rows)
        dst[mine, :] = src[mine, :]

    def wait_all(buf, sem):
        part = buf.at[pl.ds(0, (n_seq - 1) * rows)]
        pltpu.make_async_copy(part, part, sem).wait()

    def prefix(src, dst, order):
        acc = jnp.zeros((rows, HD), f32)
        for s in order:
            dst[s * rows : (s + 1) * rows, :] = acc
            acc = acc + src[s * rows : (s + 1) * rows, :]

    row = lax.broadcasted_iota(jnp.int32, (BLK, BLK), 0)
    col = lax.broadcasted_iota(jnp.int32, (BLK, BLK), 1)

    loads[0].wait()
    loads[1].wait()
    for h in range(heads):
        own[h * HD : (h + 1) * HD, :] = dot(k[:, cols(h)], v[:, cols(h)], TN)
    pl.semaphore_wait(barrier, n_seq - 1 + n_head - 1)
    scatter(own, up, up_s, up_r)

    loads[2].wait()
    loads[3].wait()

    def lower(a, b, i):
        a_i = a[i * BLK : (i + 1) * BLK]
        diag = jnp.where(row >= col, dot(a_i, b[i * BLK : (i + 1) * BLK], NT), 0.0).astype(bf16)
        left = dot(a_i, b[: i * BLK], NT).astype(bf16) if i else None
        return left, diag

    def upper(a, b, j):
        a_j = a[j * BLK : (j + 1) * BLK]
        diag = jnp.where(col >= row, dot(a_j, b[j * BLK : (j + 1) * BLK], NT), 0.0).astype(bf16)
        right = dot(a_j, b[(j + 1) * BLK :], NT).astype(bf16) if j < nb - 1 else None
        return diag, right

    for h in range(heads):
        qh, kh, vh = q[:, cols(h)], k[:, cols(h)], v[:, cols(h)]
        for i in range(nb):
            left, diag = lower(qh, kh, i)
            out = dot(diag, vh[i * BLK : (i + 1) * BLK])
            if i:
                out = out + dot(left, vh[: i * BLK])
            att[i * BLK : (i + 1) * BLK, cols(h)] = out

    wait_all(up, up_r)
    prefix(up, pre, range(n_seq))
    scatter(pre, kvb, down_s, down_r)

    for h in range(heads):
        qh, kh = q[:, cols(h)], k[:, cols(h)]
        qt[h * HD : (h + 1) * HD, :] = qh.T
        for j in range(nb):
            diag, right = upper(kh, qh, j)
            st[h, j * BLK : (j + 1) * BLK, j * BLK : (j + 1) * BLK] = diag
            if j < nb - 1:
                st[h, j * BLK : (j + 1) * BLK, (j + 1) * BLK :] = right

    wait_all(kvb, down_r)
    kvlow[...] = kvb[...].astype(bf16)

    sq = jnp.zeros((toks, HD), f32)
    cross = jnp.zeros((toks, HD), f32)
    for h in range(heads):
        a = att[:, cols(h)] + dot(q[:, cols(h)], kvlow[h * HD : (h + 1) * HD, :])
        att[:, cols(h)] = a
        sq = sq + a * a
        cross = cross + dn[:, cols(h)].astype(f32) * gain_ref[:, cols(h)] * a
    ones = jnp.ones((8, 3 * HD), bf16)
    sub = lax.broadcasted_iota(jnp.int32, (8, HD), 0)
    for n, x in enumerate((sq, cross)):
        sums = dot(ones, jnp.concatenate(thirds(x), axis=1), NT)
        tile = jnp.zeros((8, HD), f32)
        for r in range(toks // HD):
            tile = jnp.where(sub == r, sums[:, r * HD : (r + 1) * HD], tile)
        stat[n * 8 : n * 8 + 8, :] = tile

    def send_stat(d, _):
        peer = lax.rem(head + d, n_head)
        pltpu.make_async_remote_copy(
            src_ref=stat, dst_ref=stat_in.at[head],
            send_sem=stat_s, recv_sem=stat_r, device_id={"head": peer}, device_id_type=MESH,
        ).start()
        return 0

    lax.fori_loop(1, n_head, send_stat, 0)
    stat_in[head] = stat[...]
    got = stat_in.at[pl.ds(0, n_head - 1)]
    pltpu.make_async_copy(got, got, stat_r).wait()
    total = stat_in[0]
    for p in range(1, n_head):
        total = total + stat_in[p]
    features = feat * n_head
    inv = lax.rsqrt(total[:8] / features + eps)
    coef = inv * inv * inv * (total[8:] / features)

    def per_token(tile):
        spread = jnp.concatenate([jnp.where(sub == r, tile, 0.0) for r in range(toks // HD)], axis=1)
        parts = jnp.concatenate([p.astype(f32) for p in thirds(spread)], axis=0).astype(bf16)
        return dot(parts, jnp.ones((24, HD), bf16), TN)

    inv_col = per_token(inv)
    coef_col = per_token(coef)
    for h in range(heads):
        scaled = dn[:, cols(h)].astype(f32) * gain_ref[:, cols(h)]
        d = (inv_col * scaled - att[:, cols(h)] * coef_col).astype(bf16)
        da[:, cols(h)] = d
        own2[h * HD : (h + 1) * HD, :] = dot(qt[h * HD : (h + 1) * HD, :], d)
    scatter(own2, up2, up2_s, up2_r)

    for h in range(heads):
        qh, kh, vh, dh = q[:, cols(h)], k[:, cols(h)], v[:, cols(h)], da[:, cols(h)]
        for i in range(nb):
            sl = slice(i * BLK, (i + 1) * BLK)
            left, diag = lower(dh, vh, i)
            out = dot(dh[sl], kvlow[h * HD : (h + 1) * HD, :], NT) + dot(diag, kh[sl])
            if i:
                out = out + dot(left, kh[: i * BLK])
            dq_o[sl, cols(h)] = out.astype(bf16)
    dq_out = pltpu.make_async_copy(dq_o, dq_hbm, out_sem.at[0])
    dq_out.start()

    wait_all(up2, up2_r)
    prefix(up2, pre2, reversed(range(n_seq)))
    scatter(pre2, gb, down2_s, down2_r)

    for h in range(heads):
        qh, kh, vh, dh = q[:, cols(h)], k[:, cols(h)], v[:, cols(h)], da[:, cols(h)]
        for j in range(nb):
            sl = slice(j * BLK, (j + 1) * BLK)
            diag, right = upper(vh, dh, j)
            out = dot(diag, qh[sl])
            if j < nb - 1:
                out = out + dot(right, qh[(j + 1) * BLK :])
            dk_part[sl, cols(h)] = out
            dv_part[sl, cols(h)] = dot(st[h, sl, j * BLK :], dh[j * BLK :])

    wait_all(gb, down2_r)
    for h in range(heads):
        g = gb[h * HD : (h + 1) * HD, :].astype(bf16)
        dk_o[:, cols(h)] = (dk_part[:, cols(h)] + dot(v[:, cols(h)], g, NT)).astype(bf16)
        dv_o[:, cols(h)] = (dv_part[:, cols(h)] + dot(k[:, cols(h)], g)).astype(bf16)
    dk_out = pltpu.make_async_copy(dk_o, dk_hbm, out_sem.at[1])
    dv_out = pltpu.make_async_copy(dv_o, dv_hbm, out_sem.at[2])
    dk_out.start()
    dv_out.start()
    for buf, sem in ((own, up_s), (pre, down_s), (own2, up2_s), (pre2, down2_s)):
        wait_all(buf, sem)
    pltpu.make_async_copy(got, got, stat_s).wait()
    for c in (dq_out, dk_out, dv_out):
        c.wait()


def solution(mesh):
    n_seq, n_head = mesh.shape["seq"], mesh.shape["head"]

    def local(queries, keys, values, d_normed, gain):
        toks, feat = queries.shape
        heads = feat // HD
        state = pltpu.VMEM((heads * HD, HD), f32)
        wide = pltpu.VMEM((toks, feat), bf16)
        wide32 = pltpu.VMEM((toks, feat), f32)
        anywhere = pl.BlockSpec(memory_space=pl.ANY)
        out = jax.ShapeDtypeStruct((toks, feat), bf16)
        return pl.pallas_call(
            functools.partial(kernel, n_seq, n_head),
            out_shape=(out, out, out),
            in_specs=[anywhere] * 4 + [pl.BlockSpec(memory_space=pltpu.VMEM)],
            out_specs=(anywhere,) * 3,
            scratch_shapes=[
                wide, wide, wide, wide,
                pltpu.VMEM((feat, toks), bf16),
                pltpu.VMEM((heads, toks, toks), bf16),
                wide32, wide,
                state, state, state, state, pltpu.VMEM((heads * HD, HD), bf16),
                state, state, state, state,
                wide32, wide32,
                wide, wide, wide,
                pltpu.VMEM((16, HD), f32),
                pltpu.VMEM((n_head, 16, HD), f32),
                pltpu.SemaphoreType.DMA((4,)),
                pltpu.SemaphoreType.DMA((3,)),
            ] + [pltpu.SemaphoreType.DMA] * 11,
            compiler_params=pltpu.CompilerParams(
                collective_id=0, has_side_effects=True, vmem_limit_bytes=48 * 1024 * 1024
            ),
            name="scan_and_grads",
        )(queries, keys, values, d_normed, gain.reshape(1, feat))

    in_specs = (P("seq", "head"), P("seq", "head"), P("seq", "head"), P("seq", "head"), P("head"))
    out_specs = (P("seq", "head"), P("seq", "head"), P("seq", "head"))
    return jax.shard_map(local, mesh=mesh, in_specs=in_specs, out_specs=out_specs, check_vma=False)
```

time: 260 us -> 59.5 us (0.23)
  waiting for transfers between devices: 157 us -> 0 us
  Pallas kernels: 0 us -> 52.3 us
  matrix products: 35.8 us -> 0 us
  local copies, waits for them, and re-layouts: 26.3 us -> 6.03 us
  between operations: 14.6 us -> 0.65 us
  blocking collectives: 13.2 us -> 0 us
  other arithmetic: 12.1 us -> 0 us
    all_gather x2 -> x0, waiting for transfers between devices: 157 us -> none  [the longest x1 90.5 us: local(): lax.all_gather(local_key_value[None], 'seq', axis=0, tiled=True)]
    pallas_call x0 -> x1, Pallas kernels: none -> 52.3 us  [local(): pl.pallas_call(functools.partial(kernel, n_seq, n_head), out_shape=(out,...]
    dot_general x42 -> x0, matrix products: 35.8 us -> none  [the longest x4 8.54 us: local(): jnp.dot(score_list[head_index].T, d_att_cols, preferred_element_type=jnp....]
    psum x1 -> x0, blocking collectives: 13.2 us -> none  [local(): lax.psum((jnp.sum(attended_rows * attended_rows, axis=1), jnp.sum(scaled...]
    reduce_sum x3 -> x0, other arithmetic: 9.15 us -> none  [the longest x1 4.36 us: local(): kv_before = jnp.sum(shard_part * weight[:, None, None, None], axis=0)]
    all_gather x1 -> x0, local copies, waits for them, and re-layouts: 8.96 us -> none  [local(): shard_part = lax.all_gather(own_grad[None], 'seq', axis=0, tiled=True)]
    unnamed x78 -> x9, local copies, waits for them, and re-layouts: 14.2 us -> 6.03 us
  transfers between devices with their start and end apart: 2 -> 0, of which waited for: 2 -> 0; matrix products, arithmetic and copies ran while one was open for 13% -> 0% of each run, Pallas kernels for 0% -> 0%
where the time goes in v1:
time: 59.5 us; the launch traced here: 59 us
  Pallas kernels  52.3 us (88%)
  local copies, waits for them, and re-layouts  6.03 us (10%)
  between operations  0.65 us (1%)
    pallas_call x1, Pallas kernels, local(): pl.pallas_call(functools.partial(kernel, n_seq, n_head), out_shape=(out,...  52.3 us
    unnamed x9, local copies, waits for them, and re-layouts  6.03 us

profile of v1, /device:TPU:1, one launch (start us, length us, event | category | flops | bytes accessed | tf_op | source)
XLA Modules:
  0.0 59.0 jit_solution(12861895566694758970)
XLA Ops:
  0.6 0.0 copy-start
  0.6 1.2 %copy-done = bf16[1024,512]{1,0:T(8,128)(2,1)S(1)} copy-done((bf16[1024,512]{1,0:T(8,128)(2,1)S(1)}, bf16[1024,512]{1,0:T(8,128)(2,1)}, u32[]{:S(2)}) %copy-start) | copy-done | bytes 1048600
  1.9 0.0 copy-start.1
  1.9 1.2 %copy-done.1 = bf16[1024,512]{1,0:T(8,128)(2,1)S(1)} copy-done((bf16[1024,512]{1,0:T(8,128)(2,1)S(1)}, bf16[1024,512]{1,0:T(8,128)(2,1)}, u32[]{:S(2)}) %copy-start.1) | copy-done | bytes 1048600
  3.1 0.0 copy-start.2
  3.1 0.7 %copy-done.2 = f32[512]{0:T(512)S(1)} copy-done((f32[512]{0:T(512)S(1)}, f32[512]{0:T(512)}, u32[]{:S(2)}) %copy-start.2) | copy-done | bytes 2072
  3.8 52.3 %scan_and_grads.1 = (bf16[1024,512]{1,0:T(8,128)(2,1)S(1)}, bf16[1024,512]{1,0:T(8,128)(2,1)S(1)}, bf16[1024,512]{1,0:T(8,128)(2,1)S(1)}) custom-call(bf16[1024,512]{1,0:T(8,128)(2,1)S(1)} %copy-done, bf16[1024,512]{1,0:T(8,128)(2,1)S(1)} %copy-done.1, bf16[1024,512]{1,0:T(8,128)(2,1)} %v_hbm.1, bf16[1024,512]{1,0:T(8,128)(2,1)} %dn_hbm.1, f32[1,512]{1,0:T(1,128)S(1)} %bitcast.1), custom_call_target="tpu_custom_call" | custom-call | tf_op jit(solution)/shard_map/scan_and_grads/pallas_call | solution.py:249
  56.0 1.0 %copy.11 = bf16[1024,512]{1,0:T(8,128)(2,1)} copy(bf16[1024,512]{1,0:T(8,128)(2,1)S(1)} %get-tuple-element.6) | data formatting | bytes 2097152
  57.0 1.0 %copy.12 = bf16[1024,512]{1,0:T(8,128)(2,1)} copy(bf16[1024,512]{1,0:T(8,128)(2,1)S(1)} %get-tuple-element.7) | data formatting | bytes 2097152
  58.0 1.0 %copy.13 = bf16[1024,512]{1,0:T(8,128)(2,1)} copy(bf16[1024,512]{1,0:T(8,128)(2,1)S(1)} %get-tuple-element.8) | data formatting | bytes 2097152
Async XLA Ops:
  0.6 1.2 %copy-start = (bf16[1024,512]{1,0:T(8,128)(2,1)S(1)}, bf16[1024,512]{1,0:T(8,128)(2,1)}, u32[]{:S(2)}) copy-start(bf16[1024,512]{1,0:T(8,128)(2,1)} %q_hbm.1) | copy-start | bytes 3145732
  1.9 1.2 %copy-start.1 = (bf16[1024,512]{1,0:T(8,128)(2,1)S(1)}, bf16[1024,512]{1,0:T(8,128)(2,1)}, u32[]{:S(2)}) copy-start(bf16[1024,512]{1,0:T(8,128)(2,1)} %k_hbm.1) | copy-start | bytes 3145732
  3.1 0.7 %copy-start.2 = (f32[512]{0:T(512)S(1)}, f32[512]{0:T(512)}, u32[]{:S(2)}) copy-start(f32[512]{0:T(512)} %param.9) | copy-start | bytes 6148

commit v2 on v1

v2 whole, which is shorter than its diff:
```python
import functools

import jax
import jax.numpy as jnp
from jax import lax
from jax.experimental import pallas as pl
from jax.experimental.pallas import tpu as pltpu
from jax.sharding import PartitionSpec as P

MESH = pl.DeviceIdType.MESH
HD = 128
BLK = 256
NZ = 8
CHUNKS = 2
eps = 1e-06
f32 = jnp.float32
bf16 = jnp.bfloat16

NN = (((1,), (0,)), ((), ()))
NT = (((1,), (1,)), ((), ()))
TN = (((0,), (0,)), ((), ()))


def dot(a, b, dims=NN):
    return lax.dot_general(a, b, dims, preferred_element_type=f32)


def kernel(
    n_seq, n_head,
    q_hbm, k_hbm, v_hbm, dn_hbm, gain_ref,
    dq_o, dk_o, dv_o,
    q, k, v, dn, qt, st, att, scaled, da, own, up, pre, kvb, kvlow, own2, up2, pre2, gb, dk_part, dv_part,
    sq_part, cross_part, stat, stat_in,
    in_sem, up_s, up_r, down_s, down_r, up2_s, up2_r, down2_s, down2_r, stat_s, stat_r,
):
    toks, feat = q.shape
    heads = feat // HD
    nb = toks // BLK
    hc = heads // CHUNKS
    crows = hc * HD
    rows = crows // n_seq
    ny = n_seq // NZ
    seq = lax.axis_index("seq")
    head = lax.axis_index("head")
    my_y, my_z = seq // NZ, lax.rem(seq, NZ)

    loads = [
        pltpu.make_async_copy(src, dst, in_sem.at[i])
        for i, (src, dst) in enumerate(((k_hbm, k), (v_hbm, v), (q_hbm, q), (dn_hbm, dn)))
    ]
    loads[0].start()
    loads[1].start()

    along_y = [lax.rem(my_y + d, ny) * NZ for d in range(ny)]
    along_z = [lax.rem(my_z + d, NZ) for d in range(NZ)]
    offsets = sorted(
        ((y, z) for y in range(ny) for z in range(NZ) if y or z),
        key=lambda o: -min(o[0], ny - o[0]) - min(o[1], NZ - o[1]),
    )
    peers = [along_y[y] + along_z[z] for y, z in offsets]

    barrier = pltpu.get_barrier_semaphore()

    for peer in peers:
        pl.semaphore_signal(barrier, inc=1, device_id={"seq": peer}, device_id_type=MESH)
    head_peers = [lax.rem(head + d, n_head) for d in range(1, n_head)]
    for peer in head_peers:
        pl.semaphore_signal(barrier, inc=1, device_id={"head": peer}, device_id_type=MESH)

    def cols(h):
        return slice(h * HD, (h + 1) * HD)

    def scatter(c, src, dst, send, recv):
        def at(j):
            return pl.ds(pl.multiple_of(c * crows + j * rows, rows), rows)

        for peer in peers:
            pltpu.make_async_remote_copy(
                src_ref=src.at[at(peer)], dst_ref=dst.at[at(seq)],
                send_sem=send.at[c], recv_sem=recv.at[c], device_id={"seq": peer}, device_id_type=MESH,
            ).start()
        dst[at(seq), :] = src[at(seq), :]

    def wait_all(c, buf, sem):
        part = buf.at[pl.ds(c * crows, (n_seq - 1) * rows)]
        pltpu.make_async_copy(part, part, sem.at[c]).wait()

    def prefix(c, src, dst, order):
        acc = jnp.zeros((rows, HD), f32)
        for s in order:
            sl = slice(c * crows + s * rows, c * crows + (s + 1) * rows)
            dst[sl, :] = acc
            acc = acc + src[sl, :]

    def chunk_heads(c):
        return range(c * hc, (c + 1) * hc)

    row = lax.broadcasted_iota(jnp.int32, (BLK, BLK), 0)
    col = lax.broadcasted_iota(jnp.int32, (BLK, BLK), 1)

    def lower(a, b, i):
        a_i = a[i * BLK : (i + 1) * BLK]
        diag = jnp.where(row >= col, dot(a_i, b[i * BLK : (i + 1) * BLK], NT), 0.0).astype(bf16)
        left = dot(a_i, b[: i * BLK], NT).astype(bf16) if i else None
        return left, diag

    def upper(a, b, j):
        a_j = a[j * BLK : (j + 1) * BLK]
        diag = jnp.where(col >= row, dot(a_j, b[j * BLK : (j + 1) * BLK], NT), 0.0).astype(bf16)
        right = dot(a_j, b[(j + 1) * BLK :], NT).astype(bf16) if j < nb - 1 else None
        return diag, right

    loads[0].wait()
    loads[1].wait()
    loads[2].start()
    loads[3].start()
    for h in range(heads):
        own[h * HD : (h + 1) * HD, :] = dot(k[:, cols(h)], v[:, cols(h)], TN)
    pl.semaphore_wait(barrier, n_seq - 1 + n_head - 1)
    for c in range(CHUNKS):
        scatter(c, own, up, up_s, up_r)

    loads[2].wait()
    loads[3].wait()
    for h in range(heads):
        qh, kh, vh = q[:, cols(h)], k[:, cols(h)], v[:, cols(h)]
        for i in range(nb):
            left, diag = lower(qh, kh, i)
            out = dot(diag, vh[i * BLK : (i + 1) * BLK])
            if i:
                out = out + dot(left, vh[: i * BLK])
            att[i * BLK : (i + 1) * BLK, cols(h)] = out

    for c in range(CHUNKS):
        wait_all(c, up, up_r)
        prefix(c, up, pre, range(n_seq))
        scatter(c, pre, kvb, down_s, down_r)

    for h in range(heads):
        qh, kh = q[:, cols(h)], k[:, cols(h)]
        qt[h * HD : (h + 1) * HD, :] = qh.T
        scaled[:, cols(h)] = dn[:, cols(h)].astype(f32) * gain_ref[:, cols(h)]
        for j in range(nb):
            diag, right = upper(kh, qh, j)
            st[h, j * BLK : (j + 1) * BLK, j * BLK : (j + 1) * BLK] = diag
            if j < nb - 1:
                st[h, j * BLK : (j + 1) * BLK, (j + 1) * BLK :] = right

    tiles = toks // HD
    for c in range(CHUNKS):
        wait_all(c, kvb, down_r)
        sq = cross = 0.0
        for h in chunk_heads(c):
            kvlow[h * HD : (h + 1) * HD, :] = kvb[h * HD : (h + 1) * HD, :].astype(bf16)
            a = att[:, cols(h)] + dot(q[:, cols(h)], kvlow[h * HD : (h + 1) * HD, :])
            att[:, cols(h)] = a
            sq = sq + a * a
            cross = cross + scaled[:, cols(h)] * a
        if c:
            sq = sq + sq_part[...]
            cross = cross + cross_part[...]
        if c < CHUNKS - 1:
            sq_part[...] = sq
            cross_part[...] = cross
    stat[:tiles, :] = jnp.sum(sq.reshape(tiles, HD, HD), axis=-1)
    stat[tiles:, :] = jnp.sum(cross.reshape(tiles, HD, HD), axis=-1)
    for peer in head_peers:
        pltpu.make_async_remote_copy(
            src_ref=stat, dst_ref=stat_in.at[head],
            send_sem=stat_s, recv_sem=stat_r, device_id={"head": peer}, device_id_type=MESH,
        ).start()
    stat_in[head] = stat[...]
    got = stat_in.at[pl.ds(0, n_head - 1)]
    pltpu.make_async_copy(got, got, stat_r).wait()
    total = stat_in[0]
    for i in range(1, n_head):
        total = total + stat_in[i]
    features = feat * n_head
    inv = lax.rsqrt(total[:tiles] / features + eps)
    coef = inv * inv * inv * (total[tiles:] / features)

    def per_token(tile):
        return jnp.concatenate([jnp.broadcast_to(tile[r : r + 1, :], (HD, HD)).T for r in range(tiles)], axis=0)

    inv_col = per_token(inv)
    coef_col = per_token(coef)
    for c in range(CHUNKS):
        for h in chunk_heads(c):
            d = (inv_col * scaled[:, cols(h)] - att[:, cols(h)] * coef_col).astype(bf16)
            da[:, cols(h)] = d
            own2[h * HD : (h + 1) * HD, :] = dot(qt[h * HD : (h + 1) * HD, :], d)
        scatter(c, own2, up2, up2_s, up2_r)

    for h in range(heads):
        qh, kh, vh, dh = q[:, cols(h)], k[:, cols(h)], v[:, cols(h)], da[:, cols(h)]
        for i in range(nb):
            sl = slice(i * BLK, (i + 1) * BLK)
            left, diag = lower(dh, vh, i)
            out = dot(dh[sl], kvlow[h * HD : (h + 1) * HD, :], NT) + dot(diag, kh[sl])
            if i:
                out = out + dot(left, kh[: i * BLK])
            dq_o[sl, cols(h)] = out.astype(bf16)

    for c in range(CHUNKS):
        wait_all(c, up2, up2_r)
        prefix(c, up2, pre2, reversed(range(n_seq)))
        scatter(c, pre2, gb, down2_s, down2_r)

    for h in range(heads):
        qh, vh, dh = q[:, cols(h)], v[:, cols(h)], da[:, cols(h)]
        for j in range(nb):
            sl = slice(j * BLK, (j + 1) * BLK)
            diag, right = upper(vh, dh, j)
            out = dot(diag, qh[sl])
            if j < nb - 1:
                out = out + dot(right, qh[(j + 1) * BLK :])
            dk_part[sl, cols(h)] = out
            dv_part[sl, cols(h)] = dot(st[h, sl, j * BLK :], dh[j * BLK :])

    for c in range(CHUNKS):
        wait_all(c, gb, down2_r)
        for h in chunk_heads(c):
            g = gb[h * HD : (h + 1) * HD, :].astype(bf16)
            dk_o[:, cols(h)] = (dk_part[:, cols(h)] + dot(v[:, cols(h)], g, NT)).astype(bf16)
            dv_o[:, cols(h)] = (dv_part[:, cols(h)] + dot(k[:, cols(h)], g)).astype(bf16)
    for c in range(CHUNKS):
        for buf, sem in ((own, up_s), (pre, down_s), (own2, up2_s), (pre2, down2_s)):
            wait_all(c, buf, sem)
    pltpu.make_async_copy(got, got, stat_s).wait()


def write_out(a, b, c, x, y, z, sem):
    copies = [pltpu.make_async_copy(s, d, sem.at[i]) for i, (s, d) in enumerate(((a, x), (b, y), (c, z)))]
    for copy in copies:
        copy.start()
    for copy in copies:
        copy.wait()


def solution(mesh):
    n_seq, n_head = mesh.shape["seq"], mesh.shape["head"]

    def local(queries, keys, values, d_normed, gain):
        toks, feat = queries.shape
        heads = feat // HD
        state = pltpu.VMEM((heads * HD, HD), f32)
        wide = pltpu.VMEM((toks, feat), bf16)
        wide32 = pltpu.VMEM((toks, feat), f32)
        anywhere = pl.BlockSpec(memory_space=pl.ANY)
        vmem = pl.BlockSpec(memory_space=pltpu.VMEM)
        pairs = pltpu.SemaphoreType.DMA((2,))
        grads = pl.pallas_call(
            functools.partial(kernel, n_seq, n_head),
            out_shape=(pltpu.VMEM((toks, feat), bf16),) * 3,
            in_specs=[anywhere] * 4 + [vmem],
            out_specs=(vmem,) * 3,
            scratch_shapes=[
                wide, wide, wide, wide,
                pltpu.VMEM((feat, toks), bf16),
                pltpu.VMEM((heads, toks, toks), bf16),
                wide32, wide32, wide,
                state, state, state, state, pltpu.VMEM((heads * HD, HD), bf16),
                state, state, state, state,
                wide32, wide32,
                pltpu.VMEM((toks, HD), f32), pltpu.VMEM((toks, HD), f32),
                pltpu.VMEM((2 * toks // HD, HD), f32),
                pltpu.VMEM((n_head, 2 * toks // HD, HD), f32),
                pltpu.SemaphoreType.DMA((4,)),
            ] + [pairs] * 8 + [pltpu.SemaphoreType.DMA] * 2,
            compiler_params=pltpu.CompilerParams(
                collective_id=0, has_side_effects=True, vmem_limit_bytes=58 * 1024 * 1024
            ),
            name="scan_and_grads",
        )(queries, keys, values, d_normed, gain.reshape(1, feat))
        out = jax.ShapeDtypeStruct((toks, feat), bf16)
        return pl.pallas_call(
            write_out,
            out_shape=(out,) * 3,
            in_specs=[vmem] * 3,
            out_specs=(anywhere,) * 3,
            scratch_shapes=[pltpu.SemaphoreType.DMA((3,))],
            compiler_params=pltpu.CompilerParams(vmem_limit_bytes=4 * 1024 * 1024),
            name="write_out",
        )(*[pltpu.with_memory_space_constraint(x, pltpu.VMEM) for x in grads])

    in_specs = (P("seq", "head"), P("seq", "head"), P("seq", "head"), P("seq", "head"), P("head"))
    out_specs = (P("seq", "head"), P("seq", "head"), P("seq", "head"))
    return jax.shard_map(local, mesh=mesh, in_specs=in_specs, out_specs=out_specs, check_vma=False)
```

time: 59.5 us -> 50.4 us (0.85)
  local copies, waits for them, and re-layouts: 6.03 us -> 0 us
  Pallas kernels: 52.3 us -> 49.4 us
    unnamed x9 -> x0, local copies, waits for them, and re-layouts: 6.03 us -> none
    pallas_call x1 -> x2, Pallas kernels: 52.3 us -> 49.4 us  [the longest x1 47.7 us: local(): pl.pallas_call(functools.partial(kernel, n_seq, n_head), out_shape=(pltpu...]
where the time goes in v2:
time: 50.4 us; the launch traced here: 50.2 us
  Pallas kernels  49.4 us (98%)
  between operations  0.8 us (2%)
    pallas_call x1, Pallas kernels, local(): pl.pallas_call(functools.partial(kernel, n_seq, n_head), out_shape=(pltpu...  47.7 us
    pallas_call x1, Pallas kernels, local(): pl.pallas_call(write_out, out_shape=(out,) * 3, in_specs=[vmem] * 3, out_...  1.69 us

profile of v2, /device:TPU:1, one launch (start us, length us, event | category | flops | bytes accessed | tf_op | source)
XLA Modules:
  0.0 50.2 jit_solution(4726586386358675477)
XLA Ops:
  0.6 47.7 %scan_and_grads.1 = (bf16[1024,512]{1,0:T(8,128)(2,1)S(1)}, bf16[1024,512]{1,0:T(8,128)(2,1)S(1)}, bf16[1024,512]{1,0:T(8,128)(2,1)S(1)}) custom-call(bf16[1024,512]{1,0:T(8,128)(2,1)} %q_hbm.1, bf16[1024,512]{1,0:T(8,128)(2,1)} %k_hbm.1, bf16[1024,512]{1,0:T(8,128)(2,1)} %v_hbm.1, bf16[1024,512]{1,0:T(8,128)(2,1)} %dn_hbm.1, f32[1,512]{1,0:T(1,128)} %bitcast.1), custom_call_target="tpu_custom_call" | custom-call | tf_op jit(solution)/shard_map/scan_and_grads/pallas_call | solution.py:252
  48.4 1.7 %write_out.1 = (bf16[1024,512]{1,0:T(8,128)(2,1)}, bf16[1024,512]{1,0:T(8,128)(2,1)}, bf16[1024,512]{1,0:T(8,128)(2,1)}) custom-call(bf16[1024,512]{1,0:T(8,128)(2,1)S(1)} %get-tuple-element.6.a, bf16[1024,512]{1,0:T(8,128)(2,1)S(1)} %get-tuple-element.7.b, bf16[1024,512]{1,0:T(8,128)(2,1)S(1)} %get-tuple-element.8.c), custom_call_target="tpu_custom_call" | custom-call | tf_op jit(solution)/shard_map/write_out/pallas_call | solution.py:276

commit v3 on v2

--- a/solution.py
+++ b/solution.py
@@ -27,10 +27,10 @@
 
 def kernel(
     n_seq, n_head,
-    q_hbm, k_hbm, v_hbm, dn_hbm, gain_ref,
-    dq_o, dk_o, dv_o,
-    q, k, v, dn, qt, st, att, scaled, da, own, up, pre, kvb, kvlow, own2, up2, pre2, gb, dk_part, dv_part,
-    sq_part, cross_part, stat, stat_in,
+    q_hbm, k_hbm, v_hbm, dn_hbm, gain_hbm,
+    dq_o, dk_o, dv_o, k, v, dk_late, dv_late, g_late,
+    q, dn, qt, st, att, scaled, da, own, up, pre, kvb, kvlow, own2, up2, pre2, gb, dk_early, dv_early,
+    gain_ref, sq_part, cross_part, stat, stat_in,
     in_sem, up_s, up_r, down_s, down_r, up2_s, up2_r, down2_s, down2_r, stat_s, stat_r,
 ):
     toks, feat = q.shape
@@ -46,15 +46,13 @@
 
     loads = [
         pltpu.make_async_copy(src, dst, in_sem.at[i])
-        for i, (src, dst) in enumerate(((k_hbm, k), (v_hbm, v), (q_hbm, q), (dn_hbm, dn)))
+        for i, (src, dst) in enumerate(((k_hbm, k), (v_hbm, v), (q_hbm, q), (dn_hbm, dn), (gain_hbm, gain_ref)))
     ]
-    loads[0].start()
-    loads[1].start()
-
+    other = head + 1 - 2 * lax.rem(head, 2)
     along_y = [lax.rem(my_y + d, ny) * NZ for d in range(ny)]
     along_z = [lax.rem(my_z + d, NZ) for d in range(NZ)]
     offsets = sorted(
-        ((y, z) for y in range(ny) for z in range(NZ) if y or z),
+        ((y, z) for y in range(ny) for z in range(NZ)),
         key=lambda o: -min(o[0], ny - o[0]) - min(o[1], NZ - o[1]),
     )
     peers = [along_y[y] + along_z[z] for y, z in offsets]
@@ -62,11 +60,14 @@
     barrier = pltpu.get_barrier_semaphore()
 
     for peer in peers:
-        pl.semaphore_signal(barrier, inc=1, device_id={"seq": peer}, device_id_type=MESH)
+        pl.semaphore_signal(barrier, inc=1, device_id={"seq": peer, "head": other}, device_id_type=MESH)
     head_peers = [lax.rem(head + d, n_head) for d in range(1, n_head)]
     for peer in head_peers:
         pl.semaphore_signal(barrier, inc=1, device_id={"head": peer}, device_id_type=MESH)
 
+    loads[0].start()
+    loads[1].start()
+
     def cols(h):
         return slice(h * HD, (h + 1) * HD)
 
@@ -77,12 +78,11 @@
         for peer in peers:
             pltpu.make_async_remote_copy(
                 src_ref=src.at[at(peer)], dst_ref=dst.at[at(seq)],
-                send_sem=send.at[c], recv_sem=recv.at[c], device_id={"seq": peer}, device_id_type=MESH,
+                send_sem=send.at[c], recv_sem=recv.at[c], device_id={"seq": peer, "head": other}, device_id_type=MESH,
             ).start()
-        dst[at(seq), :] = src[at(seq), :]
 
     def wait_all(c, buf, sem):
-        part = buf.at[pl.ds(c * crows, (n_seq - 1) * rows)]
+        part = buf.at[pl.ds(c * crows, crows)]
         pltpu.make_async_copy(part, part, sem.at[c]).wait()
 
     def prefix(c, src, dst, order):
@@ -112,17 +112,17 @@
 
     loads[0].wait()
     loads[1].wait()
-    loads[2].start()
-    loads[3].start()
+    for c in loads[2:]:
+        c.start()
     for h in range(heads):
         own[h * HD : (h + 1) * HD, :] = dot(k[:, cols(h)], v[:, cols(h)], TN)
-    pl.semaphore_wait(barrier, n_seq - 1 + n_head - 1)
+    pl.semaphore_wait(barrier, n_seq + n_head - 1)
     for c in range(CHUNKS):
         scatter(c, own, up, up_s, up_r)
 
-    loads[2].wait()
-    loads[3].wait()
-    for h in range(heads):
+    for c in loads[2:]:
+        c.wait()
+    def attend_own(h):
         qh, kh, vh = q[:, cols(h)], k[:, cols(h)], v[:, cols(h)]
         for i in range(nb):
             left, diag = lower(qh, kh, i)
@@ -131,12 +131,10 @@
                 out = out + dot(left, vh[: i * BLK])
             att[i * BLK : (i + 1) * BLK, cols(h)] = out
 
-    for c in range(CHUNKS):
-        wait_all(c, up, up_r)
-        prefix(c, up, pre, range(n_seq))
-        scatter(c, pre, kvb, down_s, down_r)
-
-    for h in range(heads):
+    for h in range(heads - 1):
+        attend_own(h)
+
+    def upper_scores(h):
         qh, kh = q[:, cols(h)], k[:, cols(h)]
         qt[h * HD : (h + 1) * HD, :] = qh.T
         scaled[:, cols(h)] = dn[:, cols(h)].astype(f32) * gain_ref[:, cols(h)]
@@ -145,6 +143,18 @@
             st[h, j * BLK : (j + 1) * BLK, j * BLK : (j + 1) * BLK] = diag
             if j < nb - 1:
                 st[h, j * BLK : (j + 1) * BLK, (j + 1) * BLK :] = right
+
+    def owner_step(src, ready, mid, back, send, recv, order, work):
+        for c in range(CHUNKS):
+            wait_all(c, src, ready)
+            prefix(c, src, mid, order)
+            scatter(c, mid, back, send, recv)
+            work[c]()
+
+    owner_step(up, up_r, pre, kvb, down_s, down_r, range(n_seq), (
+        lambda: attend_own(heads - 1),
+        lambda: [upper_scores(h) for h in range(heads)],
+    ))
 
     tiles = toks // HD
     for c in range(CHUNKS):
@@ -201,12 +211,7 @@
                 out = out + dot(left, kh[: i * BLK])
             dq_o[sl, cols(h)] = out.astype(bf16)
 
-    for c in range(CHUNKS):
-        wait_all(c, up2, up2_r)
-        prefix(c, up2, pre2, reversed(range(n_seq)))
-        scatter(c, pre2, gb, down2_s, down2_r)
-
-    for h in range(heads):
+    def upper_grads(h):
         qh, vh, dh = q[:, cols(h)], v[:, cols(h)], da[:, cols(h)]
         for j in range(nb):
             sl = slice(j * BLK, (j + 1) * BLK)
@@ -214,25 +219,51 @@
             out = dot(diag, qh[sl])
             if j < nb - 1:
                 out = out + dot(right, qh[(j + 1) * BLK :])
-            dk_part[sl, cols(h)] = out
-            dv_part[sl, cols(h)] = dot(st[h, sl, j * BLK :], dh[j * BLK :])
-
-    for c in range(CHUNKS):
-        wait_all(c, gb, down2_r)
-        for h in chunk_heads(c):
-            g = gb[h * HD : (h + 1) * HD, :].astype(bf16)
-            dk_o[:, cols(h)] = (dk_part[:, cols(h)] + dot(v[:, cols(h)], g, NT)).astype(bf16)
-            dv_o[:, cols(h)] = (dv_part[:, cols(h)] + dot(k[:, cols(h)], g)).astype(bf16)
+            dk_part, dv_part = ((dk_early, dv_early), (dk_late, dv_late))[h // hc]
+            dk_part[sl, cols(h % hc)] = out
+            dv_part[sl, cols(h % hc)] = dot(st[h, sl, j * BLK :], dh[j * BLK :])
+
+    owner_step(up2, up2_r, pre2, gb, down2_s, down2_r, range(n_seq - 1, -1, -1), (
+        lambda: upper_grads(0),
+        lambda: [upper_grads(h) for h in range(1, heads)],
+    ))
+
+    wait_all(0, gb, down2_r)
+    for h in range(hc):
+        g = gb[h * HD : (h + 1) * HD, :].astype(bf16)
+        dk_o[:, cols(h)] = (dk_early[:, cols(h)] + dot(v[:, cols(h)], g, NT)).astype(bf16)
+        dv_o[:, cols(h)] = (dv_early[:, cols(h)] + dot(k[:, cols(h)], g)).astype(bf16)
+    wait_all(1, gb, down2_r)
+    g_late[...] = gb[crows:, :].astype(bf16)
     for c in range(CHUNKS):
         for buf, sem in ((own, up_s), (pre, down_s), (own2, up2_s), (pre2, down2_s)):
             wait_all(c, buf, sem)
     pltpu.make_async_copy(got, got, stat_s).wait()
 
 
-def write_out(a, b, c, x, y, z, sem):
-    copies = [pltpu.make_async_copy(s, d, sem.at[i]) for i, (s, d) in enumerate(((a, x), (b, y), (c, z)))]
+def finish(dq, dk, dv, k, v, dk_late, dv_late, g_late, dq_hbm, dk_hbm, dv_hbm, dk_o, dv_o, early_sem, late_sem):
+    width = dk_late.shape[1]
+    early = pl.ds(0, dq.shape[1] - width)
+    copies = [
+        pltpu.make_async_copy(src, dst, early_sem.at[i])
+        for i, (src, dst) in enumerate(
+            ((dq, dq_hbm), (dk.at[:, early], dk_hbm.at[:, early]), (dv.at[:, early], dv_hbm.at[:, early]))
+        )
+    ]
     for copy in copies:
         copy.start()
+    for j in range(width // HD):
+        here = slice(j * HD, (j + 1) * HD)
+        there = slice(dq.shape[1] - width + j * HD, dq.shape[1] - width + (j + 1) * HD)
+        g = g_late[here, :]
+        dk_o[:, here] = (dk_late[:, here] + dot(v[:, there], g, NT)).astype(bf16)
+        dv_o[:, here] = (dv_late[:, here] + dot(k[:, there], g)).astype(bf16)
+        for i, (src, dst) in enumerate(((dk_o, dk_hbm), (dv_o, dv_hbm))):
+            copy = pltpu.make_async_copy(
+                src.at[:, pl.ds(j * HD, HD)], dst.at[:, pl.ds(dq.shape[1] - width + j * HD, HD)], late_sem.at[i, j]
+            )
+            copy.start()
+            copies.append(copy)
     for copy in copies:
         copy.wait()
 
@@ -246,41 +277,44 @@
         state = pltpu.VMEM((heads * HD, HD), f32)
         wide = pltpu.VMEM((toks, feat), bf16)
         wide32 = pltpu.VMEM((toks, feat), f32)
+        half32 = pltpu.VMEM((toks, feat // CHUNKS), f32)
+        half16 = pltpu.VMEM((toks, feat // CHUNKS), bf16)
         anywhere = pl.BlockSpec(memory_space=pl.ANY)
         vmem = pl.BlockSpec(memory_space=pltpu.VMEM)
         pairs = pltpu.SemaphoreType.DMA((2,))
         grads = pl.pallas_call(
             functools.partial(kernel, n_seq, n_head),
-            out_shape=(pltpu.VMEM((toks, feat), bf16),) * 3,
-            in_specs=[anywhere] * 4 + [vmem],
-            out_specs=(vmem,) * 3,
+            out_shape=(wide,) * 5 + (half32, half32, pltpu.VMEM((feat // CHUNKS, HD), bf16)),
+            in_specs=[anywhere] * 5,
+            out_specs=(vmem,) * 8,
             scratch_shapes=[
-                wide, wide, wide, wide,
+                wide, wide,
                 pltpu.VMEM((feat, toks), bf16),
                 pltpu.VMEM((heads, toks, toks), bf16),
                 wide32, wide32, wide,
                 state, state, state, state, pltpu.VMEM((heads * HD, HD), bf16),
                 state, state, state, state,
-                wide32, wide32,
+                half32, half32,
+                pltpu.VMEM((1, feat), f32),
                 pltpu.VMEM((toks, HD), f32), pltpu.VMEM((toks, HD), f32),
                 pltpu.VMEM((2 * toks // HD, HD), f32),
                 pltpu.VMEM((n_head, 2 * toks // HD, HD), f32),
-                pltpu.SemaphoreType.DMA((4,)),
+                pltpu.SemaphoreType.DMA((5,)),
             ] + [pairs] * 8 + [pltpu.SemaphoreType.DMA] * 2,
             compiler_params=pltpu.CompilerParams(
-                collective_id=0, has_side_effects=True, vmem_limit_bytes=58 * 1024 * 1024
+                collective_id=0, has_side_effects=True, vmem_limit_bytes=56 * 1024 * 1024
             ),
             name="scan_and_grads",
         )(queries, keys, values, d_normed, gain.reshape(1, feat))
         out = jax.ShapeDtypeStruct((toks, feat), bf16)
         return pl.pallas_call(
-            write_out,
+            finish,
             out_shape=(out,) * 3,
-            in_specs=[vmem] * 3,
+            in_specs=[vmem] * 8,
             out_specs=(anywhere,) * 3,
-            scratch_shapes=[pltpu.SemaphoreType.DMA((3,))],
-            compiler_params=pltpu.CompilerParams(vmem_limit_bytes=4 * 1024 * 1024),
-            name="write_out",
+            scratch_shapes=[half16, half16, pltpu.SemaphoreType.DMA((3,)), pltpu.SemaphoreType.DMA((2, feat // CHUNKS // HD))],
+            compiler_params=pltpu.CompilerParams(vmem_limit_bytes=6 * 1024 * 1024),
+            name="finish",
         )(*[pltpu.with_memory_space_constraint(x, pltpu.VMEM) for x in grads])
 
     in_specs = (P("seq", "head"), P("seq", "head"), P("seq", "head"), P("seq", "head"), P("head"))

time: 50.4 us -> 49.2 us (0.976)
  Pallas kernels: 49.4 us -> 48.3 us
    pallas_call x2, Pallas kernels: 49.4 us -> 48.3 us  [the longest x1 46.6 us: local(): pl.pallas_call(functools.partial(kernel, n_seq, n_head), out_shape=(wide,...]
where the time goes in v3:
time: 49.2 us; the launch traced here: 49.1 us
  Pallas kernels  48.3 us (98%)
  between operations  0.8 us (2%)
    pallas_call x1, Pallas kernels, local(): pl.pallas_call(functools.partial(kernel, n_seq, n_head), out_shape=(wide,...  46.6 us
    pallas_call x1, Pallas kernels, local(): pl.pallas_call(finish, out_shape=(out,) * 3, in_specs=[vmem] * 8, out_spe...  1.72 us

profile of v3, /device:TPU:1, one launch (start us, length us, event | category | flops | bytes accessed | tf_op | source)
XLA Modules:
  0.0 49.1 jit_solution(16141540271299104167)
XLA Ops:
  0.6 46.6 %scan_and_grads.1 = (bf16[1024,512]{1,0:T(8,128)(2,1)S(1)}, bf16[1024,512]{1,0:T(8,128)(2,1)S(1)}, bf16[1024,512]{1,0:T(8,128)(2,1)S(1)}, bf16[1024,512]{1,0:T(8...) custom-call(bf16[1024,512]{1,0:T(8,128)(2,1)} %q_hbm.1, ...), custom_call_target="tpu_custom_call" | custom-call | tf_op jit(solution)/shard_map/scan_and_grads/pallas_call | solution.py:285
  47.2 1.7 %finish.1 = (bf16[1024,512]{1,0:T(8,128)(2,1)}, bf16[1024,512]{1,0:T(8,128)(2,1)}, bf16[1024,512]{1,0:T(8,128)(2,1)}) custom-call(bf16[1024,512]{1,0:T(8,128)(2,1)S(1)} %get-tuple-element.11.dq, bf16[1024,512]{1,0:T(8,128)(2,1)S(1)} %get-tuple-element.12.dk, bf16[1024,512]{1,0:T(8,128)(2,1)S(1)} %get-tuple-element.13.dv, ...), custom_call_target="tpu_custom_call" | custom-call | tf_op jit(solution)/shard_map/finish/pallas_call | solution.py:310

commit v4 on v3

--- a/solution.py
+++ b/solution.py
@@ -9,7 +9,7 @@
 
 MESH = pl.DeviceIdType.MESH
 HD = 128
-BLK = 256
+BLK = 512
 NZ = 8
 CHUNKS = 2
 eps = 1e-06

time: 49.2 us -> 49.5 us (level)
  no operation moved by 1% of the time
where the time goes in v4:
time: 49.5 us; the launch traced here: 49.3 us
  Pallas kernels  48.5 us (98%)
  between operations  0.8 us (2%)
    pallas_call x1, Pallas kernels, local(): pl.pallas_call(functools.partial(kernel, n_seq, n_head), out_shape=(wide,...  46.8 us
    pallas_call x1, Pallas kernels, local(): pl.pallas_call(finish, out_shape=(out,) * 3, in_specs=[vmem] * 8, out_spe...  1.72 us

profile of v4, /device:TPU:1, one launch (start us, length us, event | category | flops | bytes accessed | tf_op | source)
XLA Modules:
  0.0 49.3 jit_solution(13409955690154693494)
XLA Ops:
  0.6 46.8 %scan_and_grads.1 = (bf16[1024,512]{1,0:T(8,128)(2,1)S(1)}, bf16[1024,512]{1,0:T(8,128)(2,1)S(1)}, bf16[1024,512]{1,0:T(8,128)(2,1)S(1)}, bf16[1024,512]{1,0:T(8...) custom-call(bf16[1024,512]{1,0:T(8,128)(2,1)} %q_hbm.1, ...), custom_call_target="tpu_custom_call" | custom-call | tf_op jit(solution)/shard_map/scan_and_grads/pallas_call | solution.py:285
  47.5 1.7 %finish.1 = (bf16[1024,512]{1,0:T(8,128)(2,1)}, bf16[1024,512]{1,0:T(8,128)(2,1)}, bf16[1024,512]{1,0:T(8,128)(2,1)}) custom-call(bf16[1024,512]{1,0:T(8,128)(2,1)S(1)} %get-tuple-element.11.dq, bf16[1024,512]{1,0:T(8,128)(2,1)S(1)} %get-tuple-element.12.dk, bf16[1024,512]{1,0:T(8,128)(2,1)S(1)} %get-tuple-element.13.dv, ...), custom_call_target="tpu_custom_call" | custom-call | tf_op jit(solution)/shard_map/finish/pallas_call | solution.py:310
